TPU v7x, 32 devices: a whole 2x2x4 slice. The times are simulated.
32 devices in a mesh: pix: 8 (over z, y), shell: 4 (over x, core).
Axes of the slice: x: 2, y: 2, z: 4, core: 2. Of those that a mesh axis runs over, the one named last changes fastest.
Arguments:
- field: float32 [128, 262144], P('shell', 'pix'), may hold values from -3 to 3
- momentum: float32 [128, 262144], P('shell', 'pix'), may hold values from -6 to 6
- kernels: float32 [4, 20, 128], P(None, None, 'shell'), may hold values from 0.002 to 0.02
- depth_class: int32 [262144], P('pix'), may hold values from 0 to 3
- counts: int32 [20, 262144], P(None, 'pix'), may hold values from 0 to 12
- mask: float32 [262144], P('pix'), may hold values from 0.1 to 1.5, as said below
- mean_counts: float32 [20], replicated, may hold values from 1 to 8
- shell_scale: float32 [128], P('shell'), may hold values from 0.5 to 2
Outputs:
- gradient: float32 [128, 262144], P('shell', 'pix')
- loglik: float32 [], replicated
Inputs may be any that keep to these rules, and one draw needn't show every extreme that they name: `mask`: mask weights are positive.
All inputs are finite; a program needn't handle non-finite values.
Results may differ from a plain program's by a relative error of at most 0.00005.
Values sent between devices are 32-bit elements; how exact they have to be, the bound alone decides.
A program may use at most 128 MiB of HBM per device.

v0:
```python
import jax
import jax.numpy as jnp
from jax import lax
from jax.sharding import PartitionSpec as P

CYCLE = 2048


LEAP = 0.1
ANGULAR = 0.5
RADIAL = 0.5


def padded_2(cells, sides, width):
    for axis, dim in sides:
        count = lax.axis_size(axis)
        ends = count - 1
        head = lax.slice_in_dim(cells, 0, width, axis=dim)
        tail = lax.slice_in_dim(cells, cells.shape[dim] - width, cells.shape[dim], axis=dim)
        cells = jnp.concatenate(
            [
                lax.ppermute(tail, axis, [(i, (i + 1) % count) for i in range(ends)]),
                cells,
                lax.ppermute(head, axis, [((i + 1) % count, i) for i in range(ends)]),
            ],
            axis=dim,
        )
    return cells


def shards(field, momentum, kernels, depth_class, counts, mask, mean_counts, shell_scale):
    shells_here, pixels = field.shape
    classes, bins, _ = kernels.shape
    total_pix = pixels * lax.axis_size("pix")
    position = field + LEAP * momentum
    density = jnp.exp(position)
    flat = kernels.reshape(classes * bins, shells_here)
    onehot = (depth_class[None, :] == jnp.arange(classes, dtype=jnp.int32)[:, None]).astype(
        jnp.float32
    )
    every = jnp.dot(
        flat, density, precision=lax.Precision.HIGHEST, preferred_element_type=jnp.float32
    )
    partial_proj = jnp.sum(every.reshape(classes, bins, pixels) * onehot[:, None, :], axis=0)
    counted = counts.astype(jnp.float32)
    proj = lax.psum(partial_proj, "shell")
    weighted, total = lax.psum(
        (jnp.sum(mask[None, :] * proj, axis=1), jnp.sum(counted, axis=1)), "pix"
    )
    norm = weighted / total_pix
    rate = mean_counts[:, None] * mask[None, :] * proj / norm[:, None]
    local_sum = jnp.sum(counted * jnp.log(rate) - rate)
    loglik = lax.psum(local_sum, "pix") / (bins * total_pix)
    ratio = counted / proj - (total / (total_pix * norm))[:, None] * mask[None, :]
    padded = padded_2(position, (("pix", 1),), CYCLE)
    angular = (
        4.0 * position
        - padded[:, CYCLE - 1 : CYCLE - 1 + pixels]
        - padded[:, CYCLE + 1 : CYCLE + 1 + pixels]
    )
    angular = angular - padded[:, 0:pixels] - padded[:, 2 * CYCLE : 2 * CYCLE + pixels]
    stacked = padded_2(position, (("shell", 0),), 1)
    radial = 2.0 * position - stacked[:-2] - stacked[2:]
    spread = (onehot[:, None, :] * ratio[None, :, :]).reshape(classes * bins, pixels)
    back = lax.dot_general(
        flat,
        spread,
        (((0,), (0,)), ((), ())),
        precision=lax.Precision.HIGHEST,
        preferred_element_type=jnp.float32,
    )
    like = density * back
    gradient = (
        like
        - position / (shell_scale[:, None] * shell_scale[:, None])
        - ANGULAR * angular
        - RADIAL * radial
    )
    return (gradient, loglik)


def solution(mesh):
    placed = (
        P("shell", "pix"),
        P("shell", "pix"),
        P(None, None, "shell"),
        P("pix"),
        P(None, "pix"),
        P("pix"),
        P(),
        P("shell"),
    )
    return jax.shard_map(
        shards, mesh=mesh, in_specs=placed, out_specs=(P("shell", "pix"), P()), check_vma=False
    )
```

profile of v0, /device:TPU:0, one launch (start us, length us, event | category | flops | bytes accessed | tf_op | source)
XLA Modules:
  0.0 197.4 jit_solution(10730155864228582843)
XLA Ops:
  7.2 0.0 all-reduce.3.cloned.1.call-start
  7.2 0.9 copy.11
  8.1 0.1 reshape.36
  8.2 3.9 %multiply_add_fusion = f32[32,32768]{1,0:T(8,128)S(1)} fusion(f32[32,32768]{1,0:T(8,128)} %param.8, f32[32,32768]{1,0:T(8,128)} %param.9), kind=kLoop, calls=%fused_computation.28 | loop fusion | flops 2097152 | bytes 12582912 | tf_op jit(solution)/shard_map/add | solution.py:35
  12.1 2.0 %copy-done = f32[32,32768]{1,0:T(8,128)} copy-done((f32[32,32768]{1,0:T(8,128)}, f32[32,32768]{1,0:T(8,128)S(1)}, u32[]{:S(2)}) %copy-start) | copy-done | bytes 4194328
  14.1 10.9 %convolution_bitcast_fusion = f32[80,32768]{1,0:T(8,128)} fusion(f32[80,32]{0,1:T(8,128)S(1)} %reshape.36, f32[32,32768]{1,0:T(8,128)S(1)} %multiply_add_fusion), kind=kOutput, calls=%fused_computation | convolution fusion | flops 1006632960 | bytes 14690304 | tf_op jit(solution)/shard_map/dot_general | solution.py:41
  25.1 11.4 %reshape.37 = f32[4,20,32768]{2,1,0:T(8,128)} reshape(f32[80,32768]{1,0:T(8,128)} %convolution_bitcast_fusion) | data formatting | bytes 20971520 | tf_op jit(solution)/shard_map/reshape | solution.py:44
  36.5 0.1 fusion.20
  36.6 0.8 copy-done.2
  37.4 8.0 %multiply_reduce_fusion = f32[20,32768]{1,0:T(8,128)} fusion(f32[4,20,32768]{2,1,0:T(8,128)} %reshape.37, f32[4,32768]{1,0:T(4,128)S(1)} %fusion.20), kind=kLoop, calls=%fused_computation.5 | loop fusion | flops 4587520 | bytes 13631488 | tf_op jit(solution)/shard_map/reduce_sum | solution.py:44
  45.4 0.0 all-reduce.3.cloned.1.call-update
  45.4 1.8 fusion.23
  47.3 5.6 %collective-permute-start = (f32[32,2048]{1,0:T(8,128)}, f32[32,2048]{1,0:T(8,128)}, u32[]{:S(2)}, u32[]{:S(2)}) collective-permute-start(f32[32,2048]{1,0:T(8,128)} %get-tuple-element.8), channel_id=1, source_target_pairs={{0,4},{4,8},{8,12},{12,16},{16,20},{20,24},{24,28},{1,5},{5,9},{9,... | collective-permute-start | bytes 786440 | tf_op jit(solution)/shard_map/ppermute | solution.py:22
  52.9 1.3 collective-permute-start.1
  54.1 2.4 %fusion.22 = (f32[1,32768]{1,0:T(1,128)}, f32[1,32768]{1,0:T(1,128)}) fusion(f32[32,32768]{1,0:T(8,128)} %copy-done), kind=kLoop, calls=%fused_computation.38 | loop fusion | bytes 524288 | tf_op jit(solution)/shard_map/slice | solution.py:19
  56.6 2.3 %collective-permute-start.2 = (f32[1,32768]{1,0:T(1,128)}, f32[1,32768]{1,0:T(1,128)}, u32[]{:S(2)}, u32[]{:S(2)}) collective-permute-start(f32[1,32768]{1,0:T(1,128)} %get-tuple-element.6), channel_id=1, source_target_pairs={{0,1},{1,2},{2,3},{4,5},{5,6},{6,7},{8,9},{9,10},{10,11},{12,13},{... | collective-permute-start | bytes 393224 | tf_op jit(solution)/shard_map/ppermute | solution.py:22
  58.9 1.3 collective-permute-start.3
  60.2 58.0 %all-reduce.3.cloned.1.call-done = f32[20,32768]{1,0:T(8,128)} async-done(((f32[20,32768]{1,0:T(8,128)}), f32[20,32768]{1,0:T(8,128)}) %all-reduce.3.cloned.1.call-update) | async-done | bytes 2621456 | tf_op jit(solution)/shard_map/psum | solution.py:46
  118.2 2.4 %multiply_reduce_fusion.1 = f32[20]{0:T(128)S(1)} fusion(f32[20,32768]{1,0:T(8,128)} %all-reduce.3.cloned.1.call-done, f32[32768]{0:T(1024)S(1)} %copy-done.3), kind=kLoop, calls=%fused_computation.32 | loop fusion | flops 1310700 | bytes 2752592 | tf_op jit(solution)/shard_map/reduce_sum | solution.py:48
  120.6 21.4 %psum.30 = f32[20]{0:T(128)S(1)} all-reduce(f32[20]{0:T(128)S(1)} %multiply_reduce_fusion.1), channel_id=1, replica_groups=mesh['pix'=8,'shell'=4] {'pix'}, use_global_device_ids=true, to_apply=%region_5.0 | all-reduce | flops 20 | bytes 160 | tf_op jit(solution)/shard_map/psum | solution.py:47
  142.0 3.6 %subtract_reduce_fusion = (f32[]{:T(128)}, f32[20]{0:T(128)S(1)}) fusion(f32[20,32768]{1,0:T(8,128)S(1)} %copy-done.1, s32[20,32768]{1,0:T(8,128)} %param.12, f32[20]{0:T(128)S(1)} %broadcast_multiply_fusion, f32[20]{0:T(128)S(1)} %copy-done.5, f32[32768]{0:T(1024)S(1)} %copy-done.3), kind=kLoop, calls=%fused_computation.30 | loop fusion | flops 5242859 | bytes 5374196 | tf_op jit(solution)/shard_map/reduce_sum | solution.py:52
  145.6 17.9 %all-reduce = (f32[20]{0:T(128)S(1)}, f32[]{:T(128)}) all-reduce(f32[20]{0:T(128)S(1)} %get-tuple-element.3, f32[]{:T(128)} %get-tuple-element.2), channel_id=1, replica_groups=mesh['pix'=8,'shell'=4] {'pix'}, use_global_device_ids=true, to_apply=%region_3.0 | all-reduce | flops 21 | bytes 168 | tf_op jit(solution)/shard_map/psum | solution.py:47
  163.6 4.1 %multiply_subtract_fusion = f32[20,32768]{1,0:T(8,128)} fusion(f32[20,32768]{1,0:T(8,128)S(1)} %copy-done.1, s32[20,32768]{1,0:T(8,128)} %param.12, f32[20]{0:T(128)S(1)} %div.29, f32[32768]{0:T(1024)S(1)} %copy-done.3), kind=kLoop, calls=%fused_computation.31 | loop fusion | flops 2621440 | bytes 7995472 | tf_op jit(solution)/shard_map/sub | solution.py:54
  168.4 21.0 %fusion.11 = f32[32,32768]{1,0:T(8,128)} fusion(f32[32,32768]{1,0:T(8,128)} %copy-done, f32[32,2048]{1,0:T(8,128)} %collective-permute-done.1, f32[32,2048]{1,0:T(8,128)} %collective-permute-done, f32[1,32768]{1,0:T(1,128)} %collective-permute-done.3, f32[1,32768]{1,0:T(1,128)} %collective-permute-done.2, f32[20,32768]{1,0:T(8,128)} %multiply_subtract_fusion, ...), kind=kOutput, calls=%fused_computation.18 | convolution fusion | flops 1031274496 | bytes 12331136 | tf_op jit(solution)/shard_map/dot_general | solution.py:65
  (19 shorter events, 0.0 us)
Async XLA Ops:
  7.2 111.0 %all-reduce.3.cloned.1.call-start = ((), (), s32[]{:S(2)}) async-start(), calls=%async_computation | async-start | bytes 6291456 | tf_op jit(solution)/shard_map/psum | solution.py:46
  12.1 2.0 %copy-start = (f32[32,32768]{1,0:T(8,128)}, f32[32,32768]{1,0:T(8,128)S(1)}, u32[]{:S(2)}) copy-start(f32[32,32768]{1,0:T(8,128)S(1)} %multiply_add_fusion) | copy-start | bytes 12582916
  25.1 11.4 %copy-start.4 = (s32[32768]{0:T(1024)S(1)}, s32[32768]{0:T(1024)}, u32[]{:S(2)}) copy-start(s32[32768]{0:T(1024)} %param.11) | copy-start | bytes 393220
  36.6 0.8 copy-start.2
  45.4 72.7 %copy-start.3 = (f32[32768]{0:T(1024)S(1)}, f32[32768]{0:T(1024)}, u32[]{:S(2)}) copy-start(f32[32768]{0:T(1024)} %param.13) | copy-start | bytes 393220
  45.4 75.2 %copy-start.6 = (f32[32]{0:T(128)S(1)}, f32[32]{0:T(128)}, u32[]{:S(2)}) copy-start(f32[32]{0:T(128)} %param.15) | copy-start | bytes 388
  45.4 96.6 %copy-start.5 = (f32[20]{0:T(128)S(1)}, f32[20]{0:T(128)}, u32[]{:S(2)}) copy-start(f32[20]{0:T(128)} %param.14) | copy-start | bytes 244
  47.3 121.1 %collective-permute-start = (f32[32,2048]{1,0:T(8,128)}, f32[32,2048]{1,0:T(8,128)}, u32[]{:S(2)}, u32[]{:S(2)}) collective-permute-start(f32[32,2048]{1,0:T(8,128)} %get-tuple-element.8), channel_id=1, source_target_pairs={{0,4},{4,8},{8,12},{12,16},{16,20},{20,24},{24,28},{1,5},{5,9},{9,... | collective-permute-start | bytes 786440 | tf_op jit(solution)/shard_map/ppermute | solution.py:22
  52.9 115.5 %collective-permute-start.1 = (f32[32,2048]{1,0:T(8,128)S(1)}, f32[32,2048]{1,0:T(8,128)}, u32[]{:S(2)}, u32[]{:S(2)}) collective-permute-start(f32[32,2048]{1,0:T(8,128)S(1)} %get-tuple-element.9), channel_id=1, source_target_pairs={{4,0},{8,4},{12,8},{16,12},{20,16},{24,20},{28,24},{5,1},{9,5},{13... | collective-permute-start | bytes 786440 | tf_op jit(solution)/shard_map/ppermute | solution.py:24
  56.6 111.8 %collective-permute-start.2 = (f32[1,32768]{1,0:T(1,128)}, f32[1,32768]{1,0:T(1,128)}, u32[]{:S(2)}, u32[]{:S(2)}) collective-permute-start(f32[1,32768]{1,0:T(1,128)} %get-tuple-element.6), channel_id=1, source_target_pairs={{0,1},{1,2},{2,3},{4,5},{5,6},{6,7},{8,9},{9,10},{10,11},{12,13},{... | collective-permute-start | bytes 393224 | tf_op jit(solution)/shard_map/ppermute | solution.py:22
  58.9 109.5 %collective-permute-start.3 = (f32[1,32768]{1,0:T(1,128)}, f32[1,32768]{1,0:T(1,128)}, u32[]{:S(2)}, u32[]{:S(2)}) collective-permute-start(f32[1,32768]{1,0:T(1,128)} %get-tuple-element.7), channel_id=1, source_target_pairs={{1,0},{2,1},{3,2},{5,4},{6,5},{7,6},{9,8},{10,9},{11,10},{13,12},{... | collective-permute-start | bytes 393224 | tf_op jit(solution)/shard_map/ppermute | solution.py:24
  118.2 23.8 %copy-start.1 = (f32[20,32768]{1,0:T(8,128)S(1)}, f32[20,32768]{1,0:T(8,128)}, u32[]{:S(2)}) copy-start(f32[20,32768]{1,0:T(8,128)} %all-reduce.3.cloned.1.call-done) | copy-start | bytes 7864324
Sparse Core Ops, SparseCore 0:
  45.6 72.5 all-reduce.2
where the time goes:
time: 198 us; the launch traced here: 197 us
  waiting for transfers between devices  58 us (29%)
  blocking collectives  39.3 us (20%)
  matrix products  31.9 us (16%)
  other arithmetic  22.2 us (11%)
  local copies, waits for them, and re-layouts  19.5 us (10%)
  between operations  15.9 us (8%)
  starting transfers between devices  10.5 us (5%)
    psum x1, waiting for transfers between devices, shards(): proj = lax.psum(partial_proj, 'shell')  58 us
    psum x2, blocking collectives, shards(): lax.psum((jnp.sum(mask[None, :] * proj, axis=1), jnp.sum(counted, axis=1)...  39.3 us
    dot_general x1, matrix products, shards(): lax.dot_general(flat, spread, (((0,), (0,)), ((), ())), precision=lax.Pre...  21 us
    reshape x1, local copies, waits for them, and re-layouts, shards(): every.reshape(classes, bins, pixels) * onehot[:, None, :]  11.4 us
    dot_general x1, matrix products, shards(): jnp.dot(flat, density, precision=lax.Precision.HIGHEST, preferred_element...  10.9 us
    reduce_sum x1, other arithmetic, shards(): jnp.sum(every.reshape(classes, bins, pixels) * onehot[:, None, :], axis=0)  8.02 us
    ppermute x2, starting transfers between devices, padded_2(): lax.ppermute(tail, axis, [(i, (i + 1) % count) for i in range(ends)])  7.87 us
    slice x2, local copies, waits for them, and re-layouts, padded_2(): lax.slice_in_dim(cells, cells.shape[dim] - width, cells.shape[dim], axis=...  4.26 us
  transfers between devices with their start and end apart: 5, of which 1 were waited for; matrix products, arithmetic and copies ran while one was open for 7% of the time, Pallas kernels for 0%

commit v1 on v0

v1 whole, which is shorter than its diff:
```python
import functools

import jax
import jax.numpy as jnp
from jax import lax
from jax.experimental import pallas as pl
from jax.experimental.pallas import tpu as pltpu
from jax.sharding import PartitionSpec as P

CYCLE = 2048

LEAP = 0.1
ANGULAR = 0.5
RADIAL = 0.5
MESH = pl.DeviceIdType.MESH
F32 = jnp.float32
BF16 = jnp.bfloat16
LANES = 128


def halves(value):
    high = value.astype(BF16)
    return high, (value - high.astype(F32)).astype(BF16)


def kernel(
    sizes,
    field, momentum, weight, weight_t, classes_of, counts, mask, mean, diag,
    out, loglik,
    pos, dens, part_send, part_own, part_recv, group_send, group_recv, ratio,
    low_send, high_send, low_recv, high_recv, acc, red_send, red_recv, log_send, log_recv,
    w_front, w_back,
    a_sems, b_send_sems, b_recv_sems, c_sems, halo_sems, edge_sems, red_sems, log_sems,
):
    pix_count, shell_count, classes, bins, chunk, chunks = sizes
    chips = shell_count // 2
    shells, pixels = field.shape
    padded = weight.shape[0] // classes
    half = chunk // 2
    total_pix = pixels * pix_count
    p, s = lax.axis_index("pix"), lax.axis_index("shell")
    core, chip = s % 2, s // 2

    def flip(index, step):
        return index + step - 2 * step * ((index // step) % 2)

    mate = (p, flip(s, 1))
    peers = [(p, ((chip + d) % chips) * 2 + core) for d in range(1, chips)]
    rounds = []
    step = 1
    while step < shell_count:
        rounds.append((p, flip(s, step)))
        step *= 2
    step = 1
    while step < pix_count:
        rounds.append((flip(p, step), s))
        step *= 2
    right, left = (p + 1) % pix_count, (p + pix_count - 1) % pix_count
    above, below = (s + 1) % shell_count, (s + shell_count - 1) % shell_count
    greeted = rounds + peers + [(right, s), (left, s), (p, above), (p, below)]
    barrier = pltpu.get_barrier_semaphore()
    for device in greeted:
        pl.semaphore_signal(barrier, inc=1, device_id=device, device_id_type=MESH)

    w_high, w_low = halves(weight[...])
    w_front[...] = jnp.concatenate([w_high, w_high, w_low], axis=1)
    t_high, t_low = halves(weight_t[...])
    w_back[...] = jnp.concatenate(
        [
            jnp.concatenate([t_high, t_high], axis=1),
            jnp.concatenate([t_low, jnp.zeros_like(t_low)], axis=1),
        ],
        axis=0,
    )
    acc[...] = jnp.zeros_like(acc)

    def copy_to(device, src, dst, send_sem, recv_sem):
        return pltpu.make_async_remote_copy(
            src_ref=src, dst_ref=dst, send_sem=send_sem, recv_sem=recv_sem,
            device_id=device, device_id_type=MESH,
        )

    def columns(j, lead=0):
        return pl.ds(pl.multiple_of(j * chunk + lead, LANES), chunk)

    def front(j, target):
        cols = columns(j)
        here = field[:, cols] + LEAP * momentum[:, cols]
        pos[:, columns(j, CYCLE)] = here
        low_send[:, cols] = here[0:1]
        high_send[:, cols] = here[shells - 1 : shells]
        density = jnp.exp(here)
        dens[:, cols] = density
        high, low = halves(density)
        every = jnp.dot(
            w_front[...], jnp.concatenate([high, low, high], axis=0), preferred_element_type=F32
        )
        kind = jnp.broadcast_to(classes_of[:, cols], (padded, chunk))
        part = every[:padded]
        for c in range(1, classes):
            part = jnp.where(kind == c, every[c * padded : (c + 1) * padded], part)
        target[...] = part
        acc[0] += mask[:, cols] * part
        acc[1, 0:bins] += counts[:, cols].astype(F32)

    def a_copy(k):
        return copy_to(mate, part_send.at[k], part_recv.at[k], a_sems.at[0, k], a_sems.at[1, k])

    def b_copy(k, d):
        return copy_to(
            peers[d], group_send.at[k], group_recv.at[d, k], b_send_sems.at[d, k], b_recv_sems.at[d, k]
        )

    def forward(k):
        a_copy(k).wait_recv()
        both = part_own[k] + part_recv[k]
        full = bins // 8
        for i in range(2):
            for r in range(full):
                group_send[k, i * full + r] = both[r * 8 : r * 8 + 8, i * half : (i + 1) * half]
        group_send[k, 2 * full] = jnp.concatenate(
            [both[full * 8 : bins, :half], both[full * 8 : bins, half:]], axis=0
        )
        for d in range(chips - 1):
            b_copy(k, d).start()

    other = 1 - core
    front(other * chunks, part_send.at[0])
    pl.semaphore_wait(barrier, len(greeted))
    a_copy(0).start()
    front(core * chunks, part_own.at[0])

    def front_step(k, carry):
        front(other * chunks + k, part_send.at[k])
        front(core * chunks + k, part_own.at[k])
        a_copy(k).start()
        forward(k - 1)
        return carry

    lax.fori_loop(1, chunks, front_step, 0)
    forward(chunks - 1)

    to_right = copy_to(
        (right, s), pos.at[:, pl.ds(pixels, CYCLE)], pos.at[:, pl.ds(0, CYCLE)],
        halo_sems.at[0], halo_sems.at[1],
    )
    to_left = copy_to(
        (left, s), pos.at[:, pl.ds(CYCLE, CYCLE)], pos.at[:, pl.ds(pixels + CYCLE, CYCLE)],
        halo_sems.at[2], halo_sems.at[3],
    )
    to_above = copy_to((p, above), high_send, low_recv, edge_sems.at[0], edge_sems.at[1])
    to_below = copy_to((p, below), low_send, high_recv, edge_sems.at[2], edge_sems.at[3])
    has_right, has_left = p < pix_count - 1, p > 0
    has_above, has_below = s < shell_count - 1, s > 0
    pl.when(has_right)(lambda: to_right.start())
    pl.when(has_left)(lambda: to_left.start())
    pl.when(has_above)(lambda: to_above.start())
    pl.when(has_below)(lambda: to_below.start())

    @pl.when(p == 0)
    def _():
        pos[:, 0:CYCLE] = jnp.zeros((shells, CYCLE), F32)

    @pl.when(p == pix_count - 1)
    def _():
        pos[:, pixels + CYCLE :] = jnp.zeros((shells, CYCLE), F32)

    @pl.when(s == 0)
    def _():
        low_recv[...] = jnp.zeros_like(low_recv)

    @pl.when(s == shell_count - 1)
    def _():
        high_recv[...] = jnp.zeros_like(high_recv)

    lane = lax.broadcasted_iota(jnp.int32, (padded, LANES), 1)
    weighted = jnp.sum(acc[0], axis=1, keepdims=True)
    counted = jnp.sum(acc[1], axis=1, keepdims=True) * (1.0 / shell_count)
    red_send[0] = jnp.where(lane < LANES // 2, weighted, counted)

    def butterfly(sent, received, sems):
        for i, device in enumerate(rounds):
            copy = copy_to(device, sent.at[i], received.at[i], sems.at[0, i], sems.at[1, i])
            copy.start()
            copy.wait()
            sent[i + 1] = sent[i] + received[i]

    butterfly(red_send, red_recv, red_sems)
    sums = red_send[len(rounds)]
    norm = sums[:, 0:1] * (1.0 / total_pix)
    total = sums[:, LANES - 1 : LANES]
    row = lax.broadcasted_iota(jnp.int32, (padded, 1), 0)
    norm = jnp.where(row < bins, norm, 1.0)
    coefficient = (total / (total_pix * norm))[:bins]
    acc[0] = jnp.zeros((padded, chunk), F32)

    pl.when(has_right)(lambda: to_right.wait_send())
    pl.when(has_left)(lambda: to_left.wait_send())
    pl.when(has_above)(lambda: to_above.wait_send())
    pl.when(has_below)(lambda: to_below.wait_send())
    pl.when(has_left)(lambda: to_right.wait_recv())
    pl.when(has_right)(lambda: to_left.wait_recv())
    pl.when(has_below)(lambda: to_above.wait_recv())
    pl.when(has_above)(lambda: to_below.wait_recv())

    scaled = diag[...]

    def stencil_step(j, carry):
        cols = columns(j)
        wide = pos[:, pl.ds(pl.multiple_of(j * chunk + CYCLE - LANES, LANES), chunk + 2 * LANES)]
        here = wide[:, LANES : LANES + chunk]
        around = (
            wide[:, LANES - 1 : LANES - 1 + chunk]
            + wide[:, LANES + 1 : LANES + 1 + chunk]
            + pos[:, columns(j)]
            + pos[:, columns(j, 2 * CYCLE)]
        )
        lower = jnp.concatenate([low_recv[:, cols], here[:-1]], axis=0)
        upper = jnp.concatenate([here[1:], high_recv[:, cols]], axis=0)
        out[:, cols] = ANGULAR * around + RADIAL * (lower + upper) - here * scaled
        return carry

    lax.fori_loop(0, pixels // chunk, stencil_step, 0)

    def c_copy(k):
        block = core * chunks + k
        return copy_to(mate, ratio.at[block], ratio.at[block], c_sems.at[0, k], c_sems.at[1, k])

    def unpacked(ref):
        full = bins // 8
        return jnp.concatenate(
            [
                jnp.concatenate(
                    [ref[i * full + r] for r in range(full)]
                    + [ref[2 * full][i * (bins % 8) : (i + 1) * (bins % 8)]],
                    axis=0,
                )
                for i in range(2)
            ],
            axis=1,
        )

    def back(j):
        cols = columns(j)
        kind = jnp.broadcast_to(classes_of[:, cols], (padded, chunk))
        value = ratio[j]
        high = value.astype(BF16).astype(F32)
        low = value - high
        spread = jnp.concatenate(
            [jnp.where(kind == c, x, 0.0).astype(BF16) for x in (high, low)
             for c in range(classes)],
            axis=0,
        ) if padded % 16 == 0 else jnp.concatenate(
            [jnp.where(kind == c, x, 0.0) for x in (high, low) for c in range(classes)], axis=0
        ).astype(BF16)
        both = jnp.dot(w_back[...], spread, preferred_element_type=F32)
        out[:, cols] += dens[:, cols] * (both[:shells] + both[shells:])

    def ratio_step(k, carry):
        for d in range(chips - 1):
            b_copy(k, d).wait_recv()
        block = core * chunks + k
        cols = columns(block)
        proj = unpacked(group_send.at[k])
        for d in range(chips - 1):
            proj = proj + unpacked(group_recv.at[d, k])
        number = counts[:, cols].astype(F32)
        masked = mask[:, cols]
        ratio[block, 0:bins] = number / proj - coefficient * masked
        ratio[block, bins:padded] = jnp.zeros((padded - bins, chunk), F32)
        acc[0, 0:bins] += number * jnp.log(masked * proj)
        c_copy(k).start()
        back(block)
        return carry

    def partner_step(k):
        c_copy(k).wait_recv()
        back(other * chunks + k)

    ratio_step(0, 0)

    def loop_step(k, carry):
        ratio_step(k, 0)
        partner_step(k - 1)
        return carry

    lax.fori_loop(1, chunks, loop_step, 0)
    own_log = jnp.sum(jnp.sum(acc[0], axis=1, keepdims=True), axis=0, keepdims=True)
    log_send[0] = jnp.broadcast_to(own_log * (1.0 / chips), (8, LANES))
    partner_step(chunks - 1)
    butterfly(log_send, log_recv, log_sems)

    safe_mean = jnp.where(row < bins, mean[...], 1.0)
    per_bin = jnp.where(
        row < bins, total * jnp.log(safe_mean / norm) - safe_mean * total_pix, 0.0
    )
    rest = jnp.sum(jnp.broadcast_to(per_bin, (padded, LANES)), axis=0, keepdims=True)
    loglik[...] = (log_send[len(rounds)] + rest) * (1.0 / (bins * total_pix))

    def drain(k, carry):
        a_copy(k).wait_send()
        for d in range(chips - 1):
            b_copy(k, d).wait_send()
        c_copy(k).wait_send()
        return carry

    lax.fori_loop(0, chunks, drain, 0)


def shards(pix_count, shell_count, field, momentum, kernels, depth_class, counts, mask, mean_counts, shell_scale):
    shells, pixels = field.shape
    classes, bins, _ = kernels.shape
    padded = -(-bins // 8) * 8
    assert bins % 8 == 4
    chunk = 1024
    while pixels % (2 * chunk):
        chunk //= 2
    chunks = pixels // (2 * chunk)
    chips = shell_count // 2
    weight = jnp.pad(kernels, ((0, 0), (0, padded - bins), (0, 0))).reshape(classes * padded, shells)
    mean = jnp.pad(mean_counts, (0, padded - bins), constant_values=1.0)[:, None]
    diag = (1.0 / (shell_scale * shell_scale) + 4.0 * ANGULAR + 2.0 * RADIAL)[:, None]
    steps = (pix_count.bit_length() - 1) + (shell_count.bit_length() - 1)
    tiles = 2 * (bins // 8) + 1
    vmem = pltpu.VMEM
    dma = pltpu.SemaphoreType.DMA
    edge = vmem((1, pixels), F32)
    part = vmem((chunks, padded, chunk), F32)
    scratch = [
        vmem((shells, pixels + 2 * CYCLE), F32),
        vmem((shells, pixels), F32),
        part, part, part,
        vmem((chunks, tiles, 8, chunk // 2), F32),
        vmem((chips - 1, chunks, tiles, 8, chunk // 2), F32),
        vmem((2 * chunks, padded, chunk), F32),
        edge, edge, edge, edge,
        vmem((2, padded, chunk), F32),
        vmem((steps + 1, padded, LANES), F32),
        vmem((steps, padded, LANES), F32),
        vmem((steps + 1, 8, LANES), F32),
        vmem((steps, 8, LANES), F32),
        vmem((classes * padded, 3 * shells), BF16),
        vmem((2 * shells, 2 * classes * padded), BF16),
        dma((2, chunks)),
        dma((chips - 1, chunks)),
        dma((chips - 1, chunks)),
        dma((2, chunks)),
        dma((4,)),
        dma((4,)),
        dma((2, steps)),
        dma((2, steps)),
    ]
    gradient, loglik = pl.pallas_call(
        functools.partial(kernel, (pix_count, shell_count, classes, bins, chunk, chunks)),
        out_shape=(
            jax.ShapeDtypeStruct((shells, pixels), F32),
            jax.ShapeDtypeStruct((8, LANES), F32),
        ),
        in_specs=[pl.BlockSpec(memory_space=pltpu.VMEM)] * 9,
        out_specs=(pl.BlockSpec(memory_space=pltpu.VMEM), pl.BlockSpec(memory_space=pltpu.VMEM)),
        scratch_shapes=scratch,
        compiler_params=pltpu.CompilerParams(
            collective_id=0, has_side_effects=True, vmem_limit_bytes=56 * 2**20
        ),
    )(
        field, momentum, weight, weight.T, depth_class[None, :], counts, mask[None, :], mean, diag
    )
    return gradient, loglik[0, 0]


def solution(mesh):
    placed = (
        P("shell", "pix"),
        P("shell", "pix"),
        P(None, None, "shell"),
        P("pix"),
        P(None, "pix"),
        P("pix"),
        P(),
        P("shell"),
    )
    return jax.shard_map(
        functools.partial(shards, mesh.shape["pix"], mesh.shape["shell"]),
        mesh=mesh,
        in_specs=placed,
        out_specs=(P("shell", "pix"), P()),
        check_vma=False,
    )
```

time: 198 us -> 99.4 us (0.50)
  Pallas kernels: 0 us -> 88.4 us
  waiting for transfers between devices: 58 us -> 0 us
  blocking collectives: 39.3 us -> 0 us
  matrix products: 31.9 us -> 0 us
  other arithmetic: 22.2 us -> 0.66 us
  between operations: 15.9 us -> 0.65 us
  starting transfers between devices: 10.5 us -> 0 us
  local copies, waits for them, and re-layouts: 19.5 us -> 9.39 us
    pallas_call x0 -> x1, Pallas kernels: none -> 88.4 us  [shards(): pl.pallas_call(functools.partial(kernel, (pix_count, shell_count, classes...]
    psum x1 -> x0, waiting for transfers between devices: 58 us -> none  [shards(): proj = lax.psum(partial_proj, 'shell')]
    psum x2 -> x0, blocking collectives: 39.3 us -> none  [shards(): lax.psum((jnp.sum(mask[None, :] * proj, axis=1), jnp.sum(counted, axis=1)...]
    dot_general x2 -> x0, matrix products: 31.9 us -> none  [the longest x1 21 us: shards(): lax.dot_general(flat, spread, (((0,), (0,)), ((), ())), precision=lax.Pre...]
    reduce_sum x3 -> x0, other arithmetic: 14.1 us -> none  [the longest x1 8.02 us: shards(): jnp.sum(every.reshape(classes, bins, pixels) * onehot[:, None, :], axis=0)]
    reshape x2, local copies, waits for them, and re-layouts: 11.5 us -> 0.81 us  [shards(): jnp.pad(kernels, ((0, 0), (0, padded - bins), (0, 0)))]
    ppermute x4 -> x0, starting transfers between devices: 10.4 us -> none  [the longest x2 7.87 us: padded_2(): lax.ppermute(tail, axis, [(i, (i + 1) % count) for i in range(ends)])]
    sub x1 -> x0, other arithmetic: 4.11 us -> none  [shards(): counted / proj - (total / (total_pix * norm))[:, None] * mask[None, :]]
  transfers between devices with their start and end apart: 5 -> 0, of which waited for: 1 -> 0; matrix products, arithmetic and copies ran while one was open for 7% -> 0% of each run, Pallas kernels for 0% -> 0%
where the time goes in v1:
time: 99.4 us; the launch traced here: 99.1 us
  Pallas kernels  88.4 us (89%)
  local copies, waits for them, and re-layouts  9.39 us (9%)
    pallas_call x1, Pallas kernels, shards(): pl.pallas_call(functools.partial(kernel, (pix_count, shell_count, classes...  88.4 us
    unnamed x4, local copies, waits for them, and re-layouts  5.35 us

profile of v1, /device:TPU:0, one launch (start us, length us, event | category | flops | bytes accessed | tf_op | source)
XLA Modules:
  0.0 99.1 jit_solution(13417751231147882118)
XLA Ops:
  0.6 0.7 pad_bitcast_fusion
  1.3 0.7 add_bitcast_fusion
  1.9 0.7 copy.16.mean
  2.6 0.7 copy.17.diag
  3.3 0.9 copy.18
  4.2 0.1 reshape.7
  4.3 0.0 copy-start
  4.3 0.7 copy.15.weight
  5.0 0.0 copy-done
  5.0 88.4 %shard_map.95 = (f32[32,32768]{1,0:T(8,128)}, f32[8,128]{1,0:T(8,128)}) custom-call(f32[32,32768]{1,0:T(8,128)} %field.1, f32[32,32768]{1,0:T(8,128)} %momentum.1, f32[96,32]{1,0:T(8,128)} %copy.15.weight, f32[32,96]{1,0:T(8,128)} %bitcast.10, s32[1,32768]{1,0:T(1,128)} %bitcast.11, s32[20,32768]{1,0:T(8,128)} %counts.1, f32[1,32768]{1,0:T(1,128)} %bitcast.12, ...), custom_call_target="tpu_custom_call" | custom-call | tf_op jit(solution)/shard_map/pallas_call | solution.py:353
  93.5 1.2 %slice.3 = f32[1,1]{1,0:T(1,128)} slice(f32[8,128]{1,0:T(8,128)} %get-tuple-element.5), slice={[0:1], [0:1]} | slice | bytes 8 | tf_op jit(solution)/shard_map/slice | solution.py:368
  94.7 4.5 %copy.20 = f32[32,32768]{1,0:T(8,128)} copy(f32[32,32768]{1,0:T(8,128)} %get-tuple-element.8) | data formatting | bytes 8388608
  (1 shorter events, 0.0 us)
Async XLA Ops:
  4.3 0.7 copy-start

commit v2 on v1

--- a/solution.py
+++ b/solution.py
@@ -28,9 +28,9 @@
     field, momentum, weight, weight_t, classes_of, counts, mask, mean, diag,
     out, loglik,
     pos, dens, part_send, part_own, part_recv, group_send, group_recv, ratio,
-    low_send, high_send, low_recv, high_recv, acc, red_send, red_recv, log_send, log_recv,
+    low_send, high_send, low_recv, high_recv, acc, red_send, red_recv, log_send, log_recv, shares,
     w_front, w_back,
-    a_sems, b_send_sems, b_recv_sems, c_sems, halo_sems, edge_sems, red_sems, log_sems,
+    a_sems, b_send_sems, b_recv_sems, c_sems, halo_sems, edge_sems, red_sems, log_sems, share_sems,
 ):
     pix_count, shell_count, classes, bins, chunk, chunks = sizes
     chips = shell_count // 2
@@ -55,9 +55,13 @@
     while step < pix_count:
         rounds.append((flip(p, step), s))
         step *= 2
+    log_rounds = [mate]
+    if chips > 2:
+        log_rounds += rounds[1 : shell_count.bit_length() - 1]
+    across = [((p + d) % pix_count, s) for d in range(1, pix_count)]
     right, left = (p + 1) % pix_count, (p + pix_count - 1) % pix_count
     above, below = (s + 1) % shell_count, (s + shell_count - 1) % shell_count
-    greeted = rounds + peers + [(right, s), (left, s), (p, above), (p, below)]
+    greeted = rounds[: shell_count.bit_length() - 1] + peers + across + [(p, above), (p, below)]
     barrier = pltpu.get_barrier_semaphore()
     for device in greeted:
         pl.semaphore_signal(barrier, inc=1, device_id=device, device_id_type=MESH)
@@ -87,8 +91,6 @@
         cols = columns(j)
         here = field[:, cols] + LEAP * momentum[:, cols]
         pos[:, columns(j, CYCLE)] = here
-        low_send[:, cols] = here[0:1]
-        high_send[:, cols] = here[shells - 1 : shells]
         density = jnp.exp(here)
         dens[:, cols] = density
         high, low = halves(density)
@@ -125,8 +127,15 @@
             b_copy(k, d).start()
 
     other = 1 - core
+    low_send[...] = field[0:1, :] + LEAP * momentum[0:1, :]
+    high_send[...] = field[shells - 1 : shells, :] + LEAP * momentum[shells - 1 : shells, :]
+    to_above = copy_to((p, above), high_send, low_recv, edge_sems.at[0], edge_sems.at[1])
+    to_below = copy_to((p, below), low_send, high_recv, edge_sems.at[2], edge_sems.at[3])
+    has_above, has_below = s < shell_count - 1, s > 0
     front(other * chunks, part_send.at[0])
     pl.semaphore_wait(barrier, len(greeted))
+    pl.when(has_above)(lambda: to_above.start())
+    pl.when(has_below)(lambda: to_below.start())
     a_copy(0).start()
     front(core * chunks, part_own.at[0])
 
@@ -148,14 +157,9 @@
         (left, s), pos.at[:, pl.ds(CYCLE, CYCLE)], pos.at[:, pl.ds(pixels + CYCLE, CYCLE)],
         halo_sems.at[2], halo_sems.at[3],
     )
-    to_above = copy_to((p, above), high_send, low_recv, edge_sems.at[0], edge_sems.at[1])
-    to_below = copy_to((p, below), low_send, high_recv, edge_sems.at[2], edge_sems.at[3])
     has_right, has_left = p < pix_count - 1, p > 0
-    has_above, has_below = s < shell_count - 1, s > 0
     pl.when(has_right)(lambda: to_right.start())
     pl.when(has_left)(lambda: to_left.start())
-    pl.when(has_above)(lambda: to_above.start())
-    pl.when(has_below)(lambda: to_below.start())
 
     @pl.when(p == 0)
     def _():
@@ -177,31 +181,6 @@
     weighted = jnp.sum(acc[0], axis=1, keepdims=True)
     counted = jnp.sum(acc[1], axis=1, keepdims=True) * (1.0 / shell_count)
     red_send[0] = jnp.where(lane < LANES // 2, weighted, counted)
-
-    def butterfly(sent, received, sems):
-        for i, device in enumerate(rounds):
-            copy = copy_to(device, sent.at[i], received.at[i], sems.at[0, i], sems.at[1, i])
-            copy.start()
-            copy.wait()
-            sent[i + 1] = sent[i] + received[i]
-
-    butterfly(red_send, red_recv, red_sems)
-    sums = red_send[len(rounds)]
-    norm = sums[:, 0:1] * (1.0 / total_pix)
-    total = sums[:, LANES - 1 : LANES]
-    row = lax.broadcasted_iota(jnp.int32, (padded, 1), 0)
-    norm = jnp.where(row < bins, norm, 1.0)
-    coefficient = (total / (total_pix * norm))[:bins]
-    acc[0] = jnp.zeros((padded, chunk), F32)
-
-    pl.when(has_right)(lambda: to_right.wait_send())
-    pl.when(has_left)(lambda: to_left.wait_send())
-    pl.when(has_above)(lambda: to_above.wait_send())
-    pl.when(has_below)(lambda: to_below.wait_send())
-    pl.when(has_left)(lambda: to_right.wait_recv())
-    pl.when(has_right)(lambda: to_left.wait_recv())
-    pl.when(has_below)(lambda: to_above.wait_recv())
-    pl.when(has_above)(lambda: to_below.wait_recv())
 
     scaled = diag[...]
 
@@ -215,12 +194,45 @@
             + pos[:, columns(j)]
             + pos[:, columns(j, 2 * CYCLE)]
         )
-        lower = jnp.concatenate([low_recv[:, cols], here[:-1]], axis=0)
-        upper = jnp.concatenate([here[1:], high_recv[:, cols]], axis=0)
+        lower = jnp.concatenate([jnp.zeros((1, chunk), F32), here[:-1]], axis=0)
+        upper = jnp.concatenate([here[1:], jnp.zeros((1, chunk), F32)], axis=0)
         out[:, cols] = ANGULAR * around + RADIAL * (lower + upper) - here * scaled
         return carry
 
-    lax.fori_loop(0, pixels // chunk, stencil_step, 0)
+    blocks, border = pixels // chunk, -(-CYCLE // chunk)
+    inner = max(blocks - 2 * border, 0)
+    for i, device in enumerate(rounds):
+        copy = copy_to(device, red_send.at[i], red_recv.at[i], red_sems.at[0, i], red_sems.at[1, i])
+        copy.start()
+        lax.fori_loop(
+            border + inner * i // len(rounds),
+            border + inner * (i + 1) // len(rounds),
+            stencil_step,
+            0,
+        )
+        copy.wait()
+        red_send[i + 1] = red_send[i] + red_recv[i]
+
+    sums = red_send[len(rounds)]
+    norm = sums[:, 0:1] * (1.0 / total_pix)
+    total = sums[:, LANES - 1 : LANES]
+    row = lax.broadcasted_iota(jnp.int32, (padded, 1), 0)
+    norm = jnp.where(row < bins, norm, 1.0)
+    coefficient = (total / (total_pix * norm))[:bins]
+    acc[0] = jnp.zeros((padded, chunk), F32)
+
+    pl.when(has_right)(lambda: to_right.wait_send())
+    pl.when(has_left)(lambda: to_left.wait_send())
+    pl.when(has_above)(lambda: to_above.wait_send())
+    pl.when(has_below)(lambda: to_below.wait_send())
+    pl.when(has_left)(lambda: to_right.wait_recv())
+    pl.when(has_right)(lambda: to_left.wait_recv())
+    pl.when(has_below)(lambda: to_above.wait_recv())
+    pl.when(has_above)(lambda: to_below.wait_recv())
+
+
+    lax.fori_loop(0, min(border, blocks), stencil_step, 0)
+    lax.fori_loop(max(blocks - border, border), blocks, stencil_step, 0)
 
     def c_copy(k):
         block = core * chunks + k
@@ -255,6 +267,8 @@
         ).astype(BF16)
         both = jnp.dot(w_back[...], spread, preferred_element_type=F32)
         out[:, cols] += dens[:, cols] * (both[:shells] + both[shells:])
+        out[0:1, cols] += RADIAL * low_recv[:, cols]
+        out[shells - 1 : shells, cols] += RADIAL * high_recv[:, cols]
 
     def ratio_step(k, carry):
         for d in range(chips - 1):
@@ -270,7 +284,6 @@
         ratio[block, bins:padded] = jnp.zeros((padded - bins, chunk), F32)
         acc[0, 0:bins] += number * jnp.log(masked * proj)
         c_copy(k).start()
-        back(block)
         return carry
 
     def partner_step(k):
@@ -278,24 +291,56 @@
         back(other * chunks + k)
 
     ratio_step(0, 0)
+    back(core * chunks)
 
     def loop_step(k, carry):
         ratio_step(k, 0)
+        back(core * chunks + k)
         partner_step(k - 1)
         return carry
 
-    lax.fori_loop(1, chunks, loop_step, 0)
+    lax.fori_loop(1, chunks - 1, loop_step, 0)
+    ratio_step(chunks - 1, 0)
     own_log = jnp.sum(jnp.sum(acc[0], axis=1, keepdims=True), axis=0, keepdims=True)
-    log_send[0] = jnp.broadcast_to(own_log * (1.0 / chips), (8, LANES))
+    scale = 1.0 / chips if chips > 2 else 1.0
+    log_send[0] = jnp.broadcast_to(own_log * scale, (8, LANES))
+
+    def log_copy(i):
+        return copy_to(
+            log_rounds[i], log_send.at[i], log_recv.at[i], log_sems.at[0, i], log_sems.at[1, i]
+        )
+
+    log_copy(0).start()
+    back(core * chunks + chunks - 1)
+    partner_step(chunks - 2)
+    for i in range(len(log_rounds)):
+        if i:
+            log_copy(i).start()
+        log_copy(i).wait()
+        log_send[i + 1] = log_send[i] + log_recv[i]
+    last = len(log_rounds)
+    shares[0] = log_send[last]
+
+    def share_copy(d):
+        return copy_to(
+            across[d - 1], log_send.at[last], shares.at[d], share_sems.at[0, d], share_sems.at[1, d]
+        )
+
+    for d in range(1, pix_count):
+        share_copy(d).start()
     partner_step(chunks - 1)
-    butterfly(log_send, log_recv, log_sems)
+    for d in range(1, pix_count):
+        share_copy(d).wait()
+    log_sum = shares[p]
+    for q in range(1, pix_count):
+        log_sum = log_sum + shares[(p + pix_count - q) % pix_count]
 
     safe_mean = jnp.where(row < bins, mean[...], 1.0)
     per_bin = jnp.where(
         row < bins, total * jnp.log(safe_mean / norm) - safe_mean * total_pix, 0.0
     )
     rest = jnp.sum(jnp.broadcast_to(per_bin, (padded, LANES)), axis=0, keepdims=True)
-    loglik[...] = (log_send[len(rounds)] + rest) * (1.0 / (bins * total_pix))
+    loglik[...] = (log_sum + rest) * (1.0 / (bins * total_pix))
 
     def drain(k, carry):
         a_copy(k).wait_send()
@@ -339,6 +384,7 @@
         vmem((steps, padded, LANES), F32),
         vmem((steps + 1, 8, LANES), F32),
         vmem((steps, 8, LANES), F32),
+        vmem((pix_count, 8, LANES), F32),
         vmem((classes * padded, 3 * shells), BF16),
         vmem((2 * shells, 2 * classes * padded), BF16),
         dma((2, chunks)),
@@ -349,6 +395,7 @@
         dma((4,)),
         dma((2, steps)),
         dma((2, steps)),
+        dma((2, pix_count)),
     ]
     gradient, loglik = pl.pallas_call(
         functools.partial(kernel, (pix_count, shell_count, classes, bins, chunk, chunks)),

time: 99.4 us -> 82.5 us (0.83)
  Pallas kernels: 88.4 us -> 71.6 us
    pallas_call x1, Pallas kernels: 88.4 us -> 71.6 us  [shards(): pl.pallas_call(functools.partial(kernel, (pix_count, shell_count, classes...]
where the time goes in v2:
time: 82.5 us; the launch traced here: 82.3 us
  Pallas kernels  71.6 us (87%)
  local copies, waits for them, and re-layouts  9.39 us (11%)
    pallas_call x1, Pallas kernels, shards(): pl.pallas_call(functools.partial(kernel, (pix_count, shell_count, classes...  71.6 us
    unnamed x4, local copies, waits for them, and re-layouts  5.35 us

profile of v2, /device:TPU:0, one launch (start us, length us, event | category | flops | bytes accessed | tf_op | source)
XLA Modules:
  0.0 82.3 jit_solution(3012040820950523400)
XLA Ops:
  0.6 0.7 pad_bitcast_fusion
  1.3 0.7 add_bitcast_fusion
  1.9 0.7 copy.16.mean
  2.6 0.7 copy.17.diag
  3.3 0.9 %copy.18 = f32[4,20,32]{1,0,2:T(4,128)S(1)} copy(f32[4,20,32]{2,0,1:T(4,128)} %param.10) | data formatting | bytes 20480
  4.2 0.1 reshape.7
  4.3 0.0 copy-start
  4.3 0.7 copy.15.weight
  5.0 0.0 copy-done
  5.0 71.6 %shard_map.95 = (f32[32,32768]{1,0:T(8,128)}, f32[8,128]{1,0:T(8,128)}) custom-call(f32[32,32768]{1,0:T(8,128)} %field.1, f32[32,32768]{1,0:T(8,128)} %momentum.1, f32[96,32]{1,0:T(8,128)} %copy.15.weight, f32[32,96]{1,0:T(8,128)} %bitcast.10, s32[1,32768]{1,0:T(1,128)} %bitcast.11, s32[20,32768]{1,0:T(8,128)} %counts.1, f32[1,32768]{1,0:T(1,128)} %bitcast.12, ...), custom_call_target="tpu_custom_call" | custom-call | tf_op jit(solution)/shard_map/pallas_call | solution.py:400
  76.6 1.2 %slice.3 = f32[1,1]{1,0:T(1,128)} slice(f32[8,128]{1,0:T(8,128)} %get-tuple-element.5), slice={[0:1], [0:1]} | slice | bytes 8 | tf_op jit(solution)/shard_map/slice | solution.py:415
  77.8 4.5 %copy.20 = f32[32,32768]{1,0:T(8,128)} copy(f32[32,32768]{1,0:T(8,128)} %get-tuple-element.8) | data formatting | bytes 8388608
  (1 shorter events, 0.0 us)
Async XLA Ops:
  4.3 0.7 copy-start

commit v3 on v2

--- a/solution.py
+++ b/solution.py
@@ -199,26 +199,26 @@
         out[:, cols] = ANGULAR * around + RADIAL * (lower + upper) - here * scaled
         return carry
 
+    across_chips = rounds[1 : shell_count.bit_length() - 1]
+    order = rounds[:1] + rounds[shell_count.bit_length() - 1 :] + across_chips
+    early = len(order) - 1
+
+    def red_copy(i):
+        return copy_to(
+            order[i], red_send.at[i], red_recv.at[i], red_sems.at[0, i], red_sems.at[1, i]
+        )
+
     blocks, border = pixels // chunk, -(-CYCLE // chunk)
     inner = max(blocks - 2 * border, 0)
-    for i, device in enumerate(rounds):
-        copy = copy_to(device, red_send.at[i], red_recv.at[i], red_sems.at[0, i], red_sems.at[1, i])
-        copy.start()
+    for i in range(early):
+        red_copy(i).start()
         lax.fori_loop(
-            border + inner * i // len(rounds),
-            border + inner * (i + 1) // len(rounds),
-            stencil_step,
-            0,
-        )
-        copy.wait()
+            border + inner * i // early, border + inner * (i + 1) // early, stencil_step, 0
+        )
+        red_copy(i).wait()
         red_send[i + 1] = red_send[i] + red_recv[i]
-
-    sums = red_send[len(rounds)]
-    norm = sums[:, 0:1] * (1.0 / total_pix)
-    total = sums[:, LANES - 1 : LANES]
-    row = lax.broadcasted_iota(jnp.int32, (padded, 1), 0)
-    norm = jnp.where(row < bins, norm, 1.0)
-    coefficient = (total / (total_pix * norm))[:bins]
+    red_copy(early).start()
+
     acc[0] = jnp.zeros((padded, chunk), F32)
 
     pl.when(has_right)(lambda: to_right.wait_send())
@@ -252,10 +252,45 @@
             axis=1,
         )
 
+    def ratio_step(k, carry):
+        for d in range(chips - 1):
+            b_copy(k, d).wait_recv()
+        block = core * chunks + k
+        cols = columns(block)
+        proj = unpacked(group_send.at[k])
+        for d in range(chips - 1):
+            proj = proj + unpacked(group_recv.at[d, k])
+        number = counts[:, cols].astype(F32)
+        masked = mask[:, cols]
+        ratio[block, 0:bins] = number / proj
+        ratio[block, bins:padded] = jnp.zeros((padded - bins, chunk), F32)
+        acc[0, 0:bins] += number * jnp.log(masked * proj)
+        c_copy(k).start()
+        return carry
+
+    lax.fori_loop(0, chunks, ratio_step, 0)
+    own_log = jnp.sum(jnp.sum(acc[0], axis=1, keepdims=True), axis=0, keepdims=True)
+    scale = 1.0 / chips if chips > 2 else 1.0
+    log_send[0] = jnp.broadcast_to(own_log * scale, (8, LANES))
+
+    def log_copy(i):
+        return copy_to(
+            log_rounds[i], log_send.at[i], log_recv.at[i], log_sems.at[0, i], log_sems.at[1, i]
+        )
+
+    log_copy(0).start()
+    red_copy(early).wait()
+    sums = red_send[early] + red_recv[early]
+    norm = sums[:, 0:1] * (1.0 / total_pix)
+    total = sums[:, LANES - 1 : LANES]
+    row = lax.broadcasted_iota(jnp.int32, (padded, 1), 0)
+    norm = jnp.where(row < bins, norm, 1.0)
+    coefficient = total / (total_pix * norm)
+
     def back(j):
         cols = columns(j)
         kind = jnp.broadcast_to(classes_of[:, cols], (padded, chunk))
-        value = ratio[j]
+        value = ratio[j] - coefficient * mask[:, cols]
         high = value.astype(BF16).astype(F32)
         low = value - high
         spread = jnp.concatenate(
@@ -270,49 +305,16 @@
         out[0:1, cols] += RADIAL * low_recv[:, cols]
         out[shells - 1 : shells, cols] += RADIAL * high_recv[:, cols]
 
-    def ratio_step(k, carry):
-        for d in range(chips - 1):
-            b_copy(k, d).wait_recv()
-        block = core * chunks + k
-        cols = columns(block)
-        proj = unpacked(group_send.at[k])
-        for d in range(chips - 1):
-            proj = proj + unpacked(group_recv.at[d, k])
-        number = counts[:, cols].astype(F32)
-        masked = mask[:, cols]
-        ratio[block, 0:bins] = number / proj - coefficient * masked
-        ratio[block, bins:padded] = jnp.zeros((padded - bins, chunk), F32)
-        acc[0, 0:bins] += number * jnp.log(masked * proj)
-        c_copy(k).start()
-        return carry
-
-    def partner_step(k):
+    def own_step(k, carry):
+        back(core * chunks + k)
+        return carry
+
+    def partner_step(k, carry):
         c_copy(k).wait_recv()
         back(other * chunks + k)
-
-    ratio_step(0, 0)
-    back(core * chunks)
-
-    def loop_step(k, carry):
-        ratio_step(k, 0)
-        back(core * chunks + k)
-        partner_step(k - 1)
-        return carry
-
-    lax.fori_loop(1, chunks - 1, loop_step, 0)
-    ratio_step(chunks - 1, 0)
-    own_log = jnp.sum(jnp.sum(acc[0], axis=1, keepdims=True), axis=0, keepdims=True)
-    scale = 1.0 / chips if chips > 2 else 1.0
-    log_send[0] = jnp.broadcast_to(own_log * scale, (8, LANES))
-
-    def log_copy(i):
-        return copy_to(
-            log_rounds[i], log_send.at[i], log_recv.at[i], log_sems.at[0, i], log_sems.at[1, i]
-        )
-
-    log_copy(0).start()
-    back(core * chunks + chunks - 1)
-    partner_step(chunks - 2)
+        return carry
+
+    lax.fori_loop(0, chunks, own_step, 0)
     for i in range(len(log_rounds)):
         if i:
             log_copy(i).start()
@@ -328,7 +330,7 @@
 
     for d in range(1, pix_count):
         share_copy(d).start()
-    partner_step(chunks - 1)
+    lax.fori_loop(0, chunks, partner_step, 0)
     for d in range(1, pix_count):
         share_copy(d).wait()
     log_sum = shares[p]

time: 82.5 us -> 66.9 us (0.81)
  Pallas kernels: 71.6 us -> 55.9 us
    pallas_call x1, Pallas kernels: 71.6 us -> 55.9 us  [shards(): pl.pallas_call(functools.partial(kernel, (pix_count, shell_count, classes...]
where the time goes in v3:
time: 66.9 us; the launch traced here: 66.6 us
  Pallas kernels  55.9 us (84%)
  local copies, waits for them, and re-layouts  9.39 us (14%)
    pallas_call x1, Pallas kernels, shards(): pl.pallas_call(functools.partial(kernel, (pix_count, shell_count, classes...  55.9 us
    unnamed x4, local copies, waits for them, and re-layouts  5.35 us
    broadcast_in_dim x2, local copies, waits for them, and re-layouts, shards(): jnp.pad(mean_counts, (0, padded - bins), constant_values=1.0)[:, None]  1.34 us

profile of v3, /device:TPU:0, one launch (start us, length us, event | category | flops | bytes accessed | tf_op | source)
XLA Modules:
  0.0 66.6 jit_solution(10233062257940435503)
XLA Ops:
  0.6 0.7 pad_bitcast_fusion
  1.3 0.7 add_bitcast_fusion
  1.9 0.7 %copy.16.mean = f32[24,1]{1,0:T(8,128)} copy(f32[24,1]{0,1:T(1,128)S(1)} %pad_bitcast_fusion) | data formatting | bytes 192 | tf_op jit(solution)/shard_map/broadcast_in_dim | solution.py:368
  2.6 0.7 %copy.17.diag = f32[32,1]{1,0:T(8,128)} copy(f32[32,1]{0,1:T(1,128)S(1)} %add_bitcast_fusion) | data formatting | bytes 256 | tf_op jit(solution)/shard_map/broadcast_in_dim | solution.py:369
  3.3 0.9 %copy.18 = f32[4,20,32]{1,0,2:T(4,128)S(1)} copy(f32[4,20,32]{2,0,1:T(4,128)} %param.10) | data formatting | bytes 20480
  4.2 0.1 reshape.7
  4.3 0.0 copy-start
  4.3 0.7 %copy.15.weight = f32[96,32]{1,0:T(8,128)} copy(f32[96,32]{0,1:T(8,128)S(1)} %reshape.7) | data formatting | bytes 24576 | tf_op jit(solution)/shard_map/reshape | solution.py:367
  5.0 0.0 copy-done
  5.0 55.9 %shard_map.95 = (f32[32,32768]{1,0:T(8,128)}, f32[8,128]{1,0:T(8,128)}) custom-call(f32[32,32768]{1,0:T(8,128)} %field.1, f32[32,32768]{1,0:T(8,128)} %momentum.1, f32[96,32]{1,0:T(8,128)} %copy.15.weight, f32[32,96]{1,0:T(8,128)} %bitcast.10, s32[1,32768]{1,0:T(1,128)} %bitcast.11, s32[20,32768]{1,0:T(8,128)} %counts.1, f32[1,32768]{1,0:T(1,128)} %bitcast.12, ...), custom_call_target="tpu_custom_call" | custom-call | tf_op jit(solution)/shard_map/pallas_call | solution.py:402
  61.0 1.2 %slice.3 = f32[1,1]{1,0:T(1,128)} slice(f32[8,128]{1,0:T(8,128)} %get-tuple-element.5), slice={[0:1], [0:1]} | slice | bytes 8 | tf_op jit(solution)/shard_map/slice | solution.py:417
  62.2 4.5 %copy.20 = f32[32,32768]{1,0:T(8,128)} copy(f32[32,32768]{1,0:T(8,128)} %get-tuple-element.8) | data formatting | bytes 8388608
  (1 shorter events, 0.0 us)
Async XLA Ops:
  4.3 0.7 %copy-start = (f32[96,32]{0,1:T(8,128)}, f32[96,32]{0,1:T(8,128)S(1)}, u32[]{:S(2)}) copy-start(f32[96,32]{0,1:T(8,128)S(1)} %reshape.7) | copy-start | bytes 36868
